TPU v7x, 32 devices: a whole 2x2x4 slice. The times are simulated.
32 devices in a mesh: grp: 2 (over x), req: 16 (over z, y, core).
Axes of the slice: x: 2, y: 2, z: 4, core: 2. Of those that a mesh axis runs over, the one named last changes fastest.
Arguments:
- xbc: bfloat16 [4096, 9216], P(('grp', 'req')), parts along dimension 0, may hold values from -6 to 6
- dt_raw: float32 [4096, 128], P(('grp', 'req')), parts along dimension 0, may hold values from -6 to 6
- conv_weight: float32 [4, 9216], replicated, may hold values from -3 to 3
- conv_bias: float32 [9216], replicated, may hold values from -3 to 3
- dt_bias: float32 [128], replicated, may hold values from -1 to 1
- a_log: float32 [128], replicated, may hold values from -6 to -2.5
- d_skip: float32 [128], replicated, may hold values from 0.5 to 1.5
- cache_states: bfloat16 [96, 128, 8192], P(('grp', 'req')), parts along dimension 0, may hold values from -24 to 24
- cache_tails: bfloat16 [96, 3, 9216], P(('grp', 'req')), parts along dimension 0, may hold values from -6 to 6
- hit_owner: int32 [32], P('grp'), parts along dimension 0, may hold values from 0 to 15, as said below
- hit_slot: int32 [32], P('grp'), parts along dimension 0, may hold values from 0 to 2, as said below
- hit_spans: int32 [32], P('grp'), parts along dimension 0, may hold values from 0 to 4
- request_of: int32 [32], P(('grp', 'req')), parts along dimension 0, may hold values from 0 to 15, each once
Outputs:
- y_out: bfloat16 [4096, 8192], P(('grp', 'req')), parts along dimension 0
- final_state: bfloat16 [32, 128, 8192], P(('grp', 'req')), parts along dimension 0
There are 2 independent parts, one for each index of `grp`. A program takes and returns all parts, laid end to end along the dimension named above; an argument that names none is the same for every part. Nothing has to cross between parts.
Inputs may be any that keep to these rules, and one draw needn't show every extreme that they name: `hit_owner`: owners are skewed: some devices hold the prefixes of several requests, others of none. `hit_slot`: all requests that name the same owner device name the same slot of it. `request_of`: each request stands on exactly one device.
All inputs are finite; a program needn't handle non-finite values.
Results may differ from a plain program's by a relative error of at most 0.0039.
Values may be sent and summed in bfloat16 or wider, within the bound.
A program may use at most 128 MiB of HBM per device.

v0:
```python
import jax
import jax.numpy as jnp
from jax import lax
from jax.experimental import pallas as pl
from jax.experimental.pallas import tpu as pltpu
from jax.sharding import PartitionSpec as P

HEADS = 128
HEAD_DIM = 64
GROUPS = 4
NST = 128
INNER = 8192
PER_STEP = 16
COLS = PER_STEP * HEAD_DIM
STEPS = HEADS // PER_STEP
STEPS_PER_GROUP = STEPS // GROUPS


def pick_kernel(index_ref, parts_ref, out_ref, sem):
    count = out_ref.shape[0]
    copies = []
    for i in range(count):
        copy = pltpu.make_async_copy(parts_ref.at[index_ref[i], :, pl.ds(0, INNER)], out_ref.at[i], sem.at[i])
        copy.start()
        copies.append(copy)
    for copy in copies:
        copy.wait()


def pick(parts, index):
    count = index.shape[0]
    return pl.pallas_call(
        pick_kernel,
        out_shape=jax.ShapeDtypeStruct((count, parts.shape[1], INNER), parts.dtype),
        in_specs=[pl.BlockSpec(memory_space=pltpu.SMEM), pl.BlockSpec(memory_space=pltpu.VMEM)],
        out_specs=pl.BlockSpec(memory_space=pl.ANY),
        scratch_shapes=[pltpu.SemaphoreType.DMA((count,))],
        compiler_params=pltpu.CompilerParams(vmem_limit_bytes=8 * 2**20),
        name="pick",
    )(index, parts)


def conv_block(pad, x_ref, tail_ref, w_ref, b_ref, width):
    rows = x_ref.shape[0]
    pad[0:8, 0:width] = tail_ref[...]
    pad[8 : 8 + rows, 0:width] = x_ref[...].astype(jnp.float32)
    v = jnp.broadcast_to(b_ref[...], (rows, width))
    for k in range(4):
        v = v + w_ref[k : k + 1, :] * pad[5 + k : 5 + k + rows, 0:width]
    return (v / (1.0 + jnp.exp(-v))).astype(jnp.bfloat16)


def local_kernel(
    x_ref, xb_ref, xc_ref, tx_ref, tb_ref, tc_ref, wx_ref, wb_ref, wc_ref, bx_ref, bb_ref, bc_ref,
    cum_ref, cumt_ref, stept_ref, coef_ref, skip_ref,
    y_ref, fresh_ref, c_out_ref, pad,
):
    rows = x_ref.shape[0]
    b_part = conv_block(pad, xb_ref, tb_ref, wb_ref, bb_ref, NST)
    c_part = conv_block(pad, xc_ref, tc_ref, wc_ref, bc_ref, NST)
    c_out_ref[...] = c_part
    x = conv_block(pad, x_ref, tx_ref, wx_ref, bx_ref, COLS)
    scores = lax.dot_general(c_part, b_part, (((1,), (1,)), ((), ())), preferred_element_type=jnp.float32)
    causal = lax.broadcasted_iota(jnp.int32, (rows, rows), 0) >= lax.broadcasted_iota(jnp.int32, (rows, rows), 1)
    scores = jnp.where(causal, scores, 0.0)
    low = lax.broadcasted_iota(jnp.int32, (rows, 128), 1) < HEAD_DIM
    cum = cum_ref[0]
    coef = coef_ref[0]
    zero = jnp.zeros((rows, 128), jnp.bfloat16)
    carried = []
    for j in range(0, PER_STEP, 2):
        xp = x[:, j * HEAD_DIM : (j + 2) * HEAD_DIM]
        mixes = []
        for h in (j, j + 1):
            decay = jnp.exp(jnp.minimum(cum[:, h : h + 1] - cumt_ref[0, h : h + 1, :], 0.0))
            mixes.append((scores * decay * stept_ref[0, h : h + 1, :]).astype(jnp.bfloat16))
        mix = jnp.concatenate(mixes, axis=1)
        both = jnp.concatenate([jnp.where(low, xp, zero), jnp.where(low, zero, xp)], axis=0)
        xf = xp.astype(jnp.float32)
        sl = slice(j * HEAD_DIM, (j + 2) * HEAD_DIM)
        y_ref[:, sl] = jnp.dot(mix, both, preferred_element_type=jnp.float32) + skip_ref[:, sl] * xf
        carried.append((jnp.where(low, coef[:, j : j + 1], coef[:, j + 1 : j + 2]) * xf).astype(jnp.bfloat16))
    fresh_ref[...] = lax.dot_general(
        b_part, jnp.concatenate(carried, axis=1), (((0,), (0,)), ((), ())), preferred_element_type=jnp.float32
    )


def state_kernel(live_ref, start_ref, y_ref, fresh_ref, c_ref, ecum_ref, elast_ref, y_out_ref, final_ref):
    rows = y_ref.shape[0]
    start = start_ref[...]
    start = jnp.where(live_ref[0] > 0, start, jnp.zeros_like(start))
    low = lax.broadcasted_iota(jnp.int32, (rows, 128), 1) < HEAD_DIM
    ecum = ecum_ref[0]
    ys = jnp.dot(c_ref[...], start, preferred_element_type=jnp.float32)
    for j in range(0, PER_STEP, 2):
        sl = slice(j * HEAD_DIM, (j + 2) * HEAD_DIM)
        factor = jnp.where(low, ecum[:, j : j + 1], ecum[:, j + 1 : j + 2])
        y_out_ref[:, sl] = (y_ref[:, sl] + factor * ys[:, sl]).astype(jnp.bfloat16)
    final_ref[0] = (elast_ref[...] * start.astype(jnp.float32) + fresh_ref[...]).astype(jnp.bfloat16)


def by_step(a):
    return a.reshape(a.shape[0], STEPS, PER_STEP).transpose(1, 0, 2)


def local(
    xbc, dt_raw, conv_weight, conv_bias, dt_bias, a_log, d_skip, cache_states, cache_tails,
    hit_owner, hit_slot, hit_spans, request_of,
):
    count = hit_owner.shape[0]
    rows = xbc.shape[0]
    mine = request_of[0]
    live = (hit_spans[mine] > 0).astype(jnp.int32)
    device = lax.axis_index("req")
    served = jnp.max(jnp.where(hit_owner == device, hit_slot, 0))
    send = lax.dynamic_slice_in_dim(cache_states, served, 1, 0).reshape(count, NST // count, INNER)
    number = jnp.broadcast_to(mine.astype(send.dtype), send.shape[:2] + (128,))
    parts = lax.all_to_all(
        jnp.concatenate([send, number], axis=2), "req", split_axis=0, concat_axis=0, tiled=True
    )
    every_request = parts[:, 0, INNER].astype(jnp.int32)
    own_tail = lax.dynamic_slice_in_dim(cache_tails, served, 1, 0)
    own_tail = jnp.pad(own_tail, ((0, 0), (0, 1), (0, 0)))
    every_tail = lax.all_gather(own_tail, "req", axis=0, tiled=True)[:, :3]
    owners = jnp.sum(
        jnp.where(every_request[:, None] == jnp.arange(count)[None, :], hit_owner[None, :], 0), axis=1
    )
    chosen = pick(parts, owners)
    start = lax.all_to_all(chosen, "req", split_axis=0, concat_axis=0, tiled=True).reshape(NST, INNER)

    tail = lax.dynamic_index_in_dim(every_tail, hit_owner[mine], 0, keepdims=False)
    tail = jnp.where(live > 0, tail, jnp.zeros_like(tail)).astype(jnp.float32)
    tail = jnp.pad(tail, ((5, 0), (0, 0)))
    step = jax.nn.softplus(dt_raw + dt_bias[None, :])
    below = jnp.tril(jnp.ones((rows, rows), jnp.float32))
    cum = jnp.dot(below, step * (-jnp.exp(a_log))[None, :], precision=lax.Precision.HIGHEST)
    last = cum[rows - 1]
    coef = jnp.exp(last[None, :] - cum) * step
    skip = jnp.repeat(d_skip, HEAD_DIM)[None, :]
    elast = jnp.repeat(jnp.exp(last), HEAD_DIM)[None, :]
    cumt = cum.T.reshape(STEPS, PER_STEP, rows)
    stept = step.T.reshape(STEPS, PER_STEP, rows)
    bias = conv_bias[None, :]

    first_b, first_c = INNER // NST, INNER // NST + GROUPS
    per = STEPS_PER_GROUP
    triple = lambda r: [
        pl.BlockSpec((r, COLS), lambda i: (0, i)),
        pl.BlockSpec((r, NST), lambda i: (0, first_b + i // per)),
        pl.BlockSpec((r, NST), lambda i: (0, first_c + i // per)),
    ]
    wide = lambda r: pl.BlockSpec((r, COLS), lambda i: (0, i))
    tall = pl.BlockSpec((1, rows, PER_STEP), lambda i: (i, 0, 0))
    flat = pl.BlockSpec((1, PER_STEP, rows), lambda i: (i, 0, 0))
    group = pl.BlockSpec((rows, NST), lambda i: (0, i // per))
    y_local, fresh, c_part = pl.pallas_call(
        local_kernel,
        grid=(STEPS,),
        out_shape=(
            jax.ShapeDtypeStruct((rows, INNER), jnp.float32),
            jax.ShapeDtypeStruct((NST, INNER), jnp.float32),
            jax.ShapeDtypeStruct((rows, GROUPS * NST), jnp.bfloat16),
        ),
        in_specs=triple(rows) + triple(8) + triple(4) + triple(1) + [tall, flat, flat, tall, wide(1)],
        out_specs=(wide(rows), wide(NST), group),
        scratch_shapes=[pltpu.VMEM((8 + rows, COLS), jnp.float32)],
        compiler_params=pltpu.CompilerParams(vmem_limit_bytes=58 * 2**20),
        cost_estimate=pl.CostEstimate(flops=10**9, bytes_accessed=40 * 10**6, transcendentals=4 * 10**6),
        name="local",
    )(xbc, xbc, xbc, tail, tail, tail, conv_weight, conv_weight, conv_weight, bias, bias, bias,
      by_step(cum), cumt, stept, by_step(coef), skip)

    return pl.pallas_call(
        state_kernel,
        grid=(STEPS,),
        out_shape=(
            jax.ShapeDtypeStruct((rows, INNER), jnp.bfloat16),
            jax.ShapeDtypeStruct((1, NST, INNER), jnp.bfloat16),
        ),
        in_specs=[pl.BlockSpec(memory_space=pltpu.SMEM), wide(NST), wide(rows), wide(NST), group, tall, wide(1)],
        out_specs=(wide(rows), pl.BlockSpec((1, NST, COLS), lambda i: (0, 0, i))),
        compiler_params=pltpu.CompilerParams(vmem_limit_bytes=58 * 2**20),
        name="state",
    )(live[None], start, y_local, fresh, c_part, by_step(jnp.exp(cum)), elast)


def solution(mesh):
    rows = P(("grp", "req"), None)
    slots = P(("grp", "req"), None, None)
    in_specs = (
        rows, rows, P(), P(), P(), P(), P(), slots, slots, P("grp"), P("grp"), P("grp"), P(("grp", "req")),
    )
    return jax.shard_map(local, mesh=mesh, in_specs=in_specs, out_specs=(rows, slots), check_vma=False)
```

profile of v0, /device:TPU:15, one launch (start us, length us, event | category | flops | bytes accessed | tf_op | source)
XLA Modules:
  0.0 150.6 jit_solution(16106519762662239522)
XLA Ops:
  7.2 0.0 copy-start
  7.9 1.3 fusion.7
  11.1 1.7 %dynamic-slice_bitcast_fusion = bf16[16,8,8192]{2,1,0:T(8,128)(2,1)S(1)} fusion(bf16[3,128,8192]{2,1,0:T(8,128)(2,1)} %param.20, s32[]{:T(128)S(6)} %select_n.39), kind=kLoop, calls=%fused_computation | loop fusion | bytes 4194308 | tf_op jit(solution)/shard_map/reshape | solution.py:116
  12.9 1.5 %concatenate.3 = bf16[16,8,8320]{2,1,0:T(8,128)(2,1)} pad(bf16[16,8,8192]{2,1,0:T(8,128)(2,1)S(1)} %dynamic-slice_bitcast_fusion, bf16[]{:T(256)S(6)} %convert_element_type.26), padding=0_0x0_0x0_128 | pad | bytes 4227074 | tf_op jit(solution)/shard_map/concatenate | solution.py:119
  14.4 6.7 %all-to-all-start = ((bf16[16,8,8320]{2,1,0:T(8,128)(2,1)}), bf16[16,8,8320]{2,1,0:T(8,128)(2,1)S(1)}, u32[]{:S(2)}, u32[]{:S(2)}) async-start(bf16[16,8,8320]{2,1,0:T(8,128)(2,1)} %concatenate.3), calls=%async_computation | async-start | bytes 4259840 | tf_op jit(solution)/shard_map/all_to_all | solution.py:118
  21.1 0.0 all-gather.2.cloned.1.call-start
  21.1 0.0 copy-done
  21.2 0.7 pad.11
  21.8 0.0 all-gather.2.cloned.1.call-update
  21.8 54.7 %all-to-all-done.parts_ref = bf16[16,8,8320]{2,1,0:T(8,128)(2,1)S(1)} async-done(((bf16[16,8,8320]{2,1,0:T(8,128)(2,1)}), bf16[16,8,8320]{2,1,0:T(8,128)(2,1)S(1)}, u32[]{:S(2)}, u32[]{:S(2)}) %all-to-all-start) | async-done | bytes 2129952 | tf_op jit(solution)/shard_map/all_to_all | solution.py:118
  76.6 0.4 fusion.6
  77.0 0.0 copy-done.8
  77.0 0.2 select_reduce_fusion.index_ref
  77.2 3.5 %pick.1 = bf16[16,8,8192]{2,1,0:T(8,128)(2,1)S(1)} custom-call(s32[16]{0:T(128)S(1)} %select_reduce_fusion.index_ref, bf16[16,8,8320]{2,1,0:T(8,128)(2,1)S(1)} %all-to-all-done.parts_ref), custom_call_target="tpu_custom_call" | custom-call | tf_op jit(solution)/shard_map/pick/pallas_call | solution.py:32
  80.6 0.0 copy-start.1
  80.7 1.3 copy-done.1
  82.0 0.0 copy-start.7
  82.0 4.1 %all-to-all-start.1 = ((bf16[16,8,8192]{2,1,0:T(8,128)(2,1)}), bf16[16,8,8192]{2,1,0:T(8,128)(2,1)S(1)}, u32[]{:S(2)}, u32[]{:S(2)}) async-start(bf16[16,8,8192]{2,1,0:T(8,128)(2,1)} %copy-done.1), calls=%async_computation.1 | async-start | bytes 4194304 | tf_op jit(solution)/shard_map/all_to_all | solution.py:129
  86.1 0.6 dynamic_slice.19
  87.8 0.0 copy-done.9
  87.8 0.6 dynamic_slice.16
  89.1 0.0 copy-done.5
  89.1 0.1 copy.24
  89.2 0.0 copy-done.10
  89.2 0.0 copy-done.6
  89.2 0.1 compare_select_fusion
  89.4 0.0 copy-start.4
  89.4 0.3 fusion
  89.6 0.0 copy-start.3
  89.6 0.2 slice_reduce_fusion
  89.8 0.1 broadcast_in_dim.50
  89.9 0.7 broadcast_in_dim_reshape.7.elast_ref
  90.6 0.0 copy-done.7
  90.6 0.1 broadcast_in_dim.49
  90.7 0.7 broadcast_in_dim_reshape.6.skip_ref
  91.4 0.1 fusion.10
  91.6 1.0 copy.26
  92.6 1.0 copy.27
  93.6 1.0 copy.25
  95.2 0.0 all-gather.2.cloned.1.call-done
  95.2 0.9 select_bitcast_fusion
  96.1 0.8 pad_convert_fusion.tx_ref.tb_ref.tc_ref
  96.9 0.0 copy-done.4
  96.9 0.0 copy-done.3
  96.9 13.3 %local.1 = (f32[128,8192]{1,0:T(8,128)}, f32[128,8192]{1,0:T(8,128)}, bf16[128,512]{1,0:T(8,128)(2,1)}) custom-call(bf16[128,9216]{1,0:T(8,128)(2,1)} %xc_ref.1, bf16[128,9216]{1,0:T(8,128)(2,1)} %xc_ref.1, bf16[128,9216]{1,0:T(8,128)(2,1)} %xc_ref.1, f32[8,9216]{1,0:T(8,128)} %pad_convert_fusion.tx_ref.tb_ref.tc_ref, ...), custom_call_target="tpu_custom_call" | custom-call | flops 1000000000 | bytes 40000000 | tf_op jit(solution)/shard_map/local/pallas_call | solution.py:156
  110.3 23.3 %all-to-all-done.1 = bf16[16,8,8192]{2,1,0:T(8,128)(2,1)S(1)} async-done(((bf16[16,8,8192]{2,1,0:T(8,128)(2,1)}), bf16[16,8,8192]{2,1,0:T(8,128)(2,1)S(1)}, u32[]{:S(2)}, u32[]{:S(2)}) %all-to-all-start.1) | async-done | bytes 2097184 | tf_op jit(solution)/shard_map/all_to_all | solution.py:129
  133.5 1.4 copy-done.2
  134.9 8.9 %state.1 = (bf16[128,8192]{1,0:T(8,128)(2,1)}, bf16[1,128,8192]{2,1,0:T(8,128)(2,1)}) custom-call(s32[1]{0:T(128)S(6)} %convert_element_type.25.live_ref, bf16[128,8192]{1,0:T(8,128)(2,1)} %bitcast.26, f32[128,8192]{1,0:T(8,128)} %get-tuple-element.5.y_ref, f32[128,8192]{1,0:T(8,128)} %get-tuple-element.6.fresh_ref, ...), custom_call_target="tpu_custom_call" | custom-call | tf_op jit(solution)/shard_map/state/pallas_call | solution.py:173
  (9 shorter events, 0.1 us)
Async XLA Ops:
  7.2 13.9 %copy-start = (bf16[3,3,9216]{2,1,0:T(4,128)(2,1)S(1)}, bf16[3,3,9216]{2,1,0:T(4,128)(2,1)}, u32[]{:S(2)}) copy-start(bf16[3,3,9216]{2,1,0:T(4,128)(2,1)} %param.21) | copy-start | bytes 497668
  14.4 62.6 %copy-start.8 = (s32[16]{0:T(128)S(1)}, s32[16]{0:T(128)}, u32[]{:S(2)}) copy-start(s32[16]{0:T(128)} %param.22) | copy-start | bytes 196
  14.4 62.2 %all-to-all-start = ((bf16[16,8,8320]{2,1,0:T(8,128)(2,1)}), bf16[16,8,8320]{2,1,0:T(8,128)(2,1)S(1)}, u32[]{:S(2)}, u32[]{:S(2)}) async-start(bf16[16,8,8320]{2,1,0:T(8,128)(2,1)} %concatenate.3), calls=%async_computation | async-start | bytes 4259840 | tf_op jit(solution)/shard_map/all_to_all | solution.py:118
  21.1 74.1 %all-gather.2.cloned.1.call-start = ((), (), s32[]{:S(2)}) async-start(), calls=%async_computation.2 | async-start | bytes 1253376 | tf_op jit(solution)/shard_map/all_gather | solution.py:124
  80.6 1.3 copy-start.1
  82.0 5.9 %copy-start.9 = (s32[16]{0:T(128)S(1)}, s32[16]{0:T(128)}, u32[]{:S(2)}) copy-start(s32[16]{0:T(128)} %param.24) | copy-start | bytes 196
  82.0 7.1 %copy-start.5 = (f32[128,128]{1,0:T(8,128)S(1)}, f32[128,128]{1,0:T(8,128)}, u32[]{:S(2)}) copy-start(f32[128,128]{1,0:T(8,128)} %param.14) | copy-start | bytes 196612
  82.0 7.2 %copy-start.10 = (f32[128]{0:T(128)S(1)}, f32[128]{0:T(128)}, u32[]{:S(2)}) copy-start(f32[128]{0:T(128)} %param.18) | copy-start | bytes 1540
  82.0 7.2 %copy-start.6 = (f32[128]{0:T(128)S(1)}, f32[128]{0:T(128)}, u32[]{:S(2)}) copy-start(f32[128]{0:T(128)} %param.17) | copy-start | bytes 1540
  82.0 8.6 %copy-start.7 = (f32[128]{0:T(128)S(1)}, f32[128]{0:T(128)}, u32[]{:S(2)}) copy-start(f32[128]{0:T(128)} %param.19) | copy-start | bytes 1540
  82.0 51.5 %all-to-all-start.1 = ((bf16[16,8,8192]{2,1,0:T(8,128)(2,1)}), bf16[16,8,8192]{2,1,0:T(8,128)(2,1)S(1)}, u32[]{:S(2)}, u32[]{:S(2)}) async-start(bf16[16,8,8192]{2,1,0:T(8,128)(2,1)} %copy-done.1), calls=%async_computation.1 | async-start | bytes 4194304 | tf_op jit(solution)/shard_map/all_to_all | solution.py:129
  89.4 7.6 %copy-start.4 = (f32[128,128]{0,1:T(8,128)}, f32[128,128]{0,1:T(8,128)S(1)}, u32[]{:S(2)}) copy-start(f32[128,128]{0,1:T(8,128)S(1)} %compare_select_fusion) | copy-start | bytes 196612
  89.6 7.3 %copy-start.3 = (f32[128,128]{0,1:T(8,128)}, f32[128,128]{0,1:T(8,128)S(1)}, u32[]{:S(2)}) copy-start(f32[128,128]{0,1:T(8,128)S(1)} %fusion) | copy-start | bytes 196612
  133.5 1.4 copy-start.2
Sparse Core Ops, SparseCore 0:
  24.2 54.1 all-gather.1
where the time goes:
time: 151 us
  waiting for transfers between devices  78.1 us (52%)
  Pallas kernels  25.7 us (17%)
  between operations  19.2 us (13%)
  local copies, waits for them, and re-layouts  12.8 us (8%)
  starting transfers between devices  10.8 us (7%)
  other arithmetic  3.81 us (3%)
    all_to_all x1, waiting for transfers between devices, local(): lax.all_to_all(jnp.concatenate([send, number], axis=2), 'req', split_axis...  54.7 us
    all_to_all x1, waiting for transfers between devices, local(): lax.all_to_all(chosen, 'req', split_axis=0, concat_axis=0, tiled=True)  23.3 us
    pallas_call x1, Pallas kernels, local(): pl.pallas_call(local_kernel, grid=(STEPS,), out_shape=(jax.ShapeDtypeStru...  13.3 us
    pallas_call x1, Pallas kernels, local(): pl.pallas_call(state_kernel, grid=(STEPS,), out_shape=(jax.ShapeDtypeStru...  8.85 us
    all_to_all x1, starting transfers between devices, local(): lax.all_to_all(jnp.concatenate([send, number], axis=2), 'req', split_axis...  6.69 us
    all_to_all x1, starting transfers between devices, local(): lax.all_to_all(chosen, 'req', split_axis=0, concat_axis=0, tiled=True)  4.11 us
    pallas_call x1, Pallas kernels, pick(): pl.pallas_call(pick_kernel, out_shape=jax.ShapeDtypeStruct((count, parts....  3.48 us
    reshape x3, local copies, waits for them, and re-layouts, by_step(): return a.reshape(a.shape[0], STEPS, PER_STEP).transpose(1, 0, 2)  3.06 us
  transfers between devices with their start and end apart: 3, of which 2 were waited for; matrix products, arithmetic and copies ran while one was open for 6% of the time, Pallas kernels for 11%

commit v1 on v0

--- a/solution.py
+++ b/solution.py
@@ -1,3 +1,5 @@
+import functools
+
 import jax
 import jax.numpy as jnp
 from jax import lax
@@ -85,30 +87,496 @@
     )
 
 
-def state_kernel(live_ref, start_ref, y_ref, fresh_ref, c_ref, ecum_ref, elast_ref, y_out_ref, final_ref):
+def state_kernel(start_ref, y_ref, fresh_ref, c_ref, ecum_ref, elast_ref, y_out_ref, final_ref):
     rows = y_ref.shape[0]
-    start = start_ref[...]
-    start = jnp.where(live_ref[0] > 0, start, jnp.zeros_like(start))
     low = lax.broadcasted_iota(jnp.int32, (rows, 128), 1) < HEAD_DIM
     ecum = ecum_ref[0]
-    ys = jnp.dot(c_ref[...], start, preferred_element_type=jnp.float32)
-    for j in range(0, PER_STEP, 2):
-        sl = slice(j * HEAD_DIM, (j + 2) * HEAD_DIM)
-        factor = jnp.where(low, ecum[:, j : j + 1], ecum[:, j + 1 : j + 2])
-        y_out_ref[:, sl] = (y_ref[:, sl] + factor * ys[:, sl]).astype(jnp.bfloat16)
-    final_ref[0] = (elast_ref[...] * start.astype(jnp.float32) + fresh_ref[...]).astype(jnp.bfloat16)
+    for half in range(COLS // CC):
+        start = start_ref[0, half]
+        here = slice(half * CC, (half + 1) * CC)
+        ys = jnp.dot(c_ref[...], start, preferred_element_type=jnp.float32)
+        for j in range(half * CC // HEAD_DIM, (half + 1) * CC // HEAD_DIM, 2):
+            sl = slice(j * HEAD_DIM, (j + 2) * HEAD_DIM)
+            factor = jnp.where(low, ecum[:, j : j + 1], ecum[:, j + 1 : j + 2])
+            inner = slice(j * HEAD_DIM - half * CC, (j + 2) * HEAD_DIM - half * CC)
+            y_out_ref[:, sl] = (y_ref[:, sl] + factor * ys[:, inner]).astype(jnp.bfloat16)
+        final_ref[0, :, here] = (
+            elast_ref[:, here] * start.astype(jnp.float32) + fresh_ref[:, here]
+        ).astype(jnp.bfloat16)
 
 
 def by_step(a):
     return a.reshape(a.shape[0], STEPS, PER_STEP).transpose(1, 0, 2)
 
 
-def local(
-    xbc, dt_raw, conv_weight, conv_bias, dt_bias, a_log, d_skip, cache_states, cache_tails,
-    hit_owner, hit_slot, hit_spans, request_of,
+LANES = 4
+CHUNKS = 4
+WIDE = INNER // LANES
+CC = WIDE // CHUNKS
+TAIL_ROWS = 16
+LAG = 2
+MESH = pl.DeviceIdType.MESH
+
+
+def masked_column(row, rows):
+    sub = lax.broadcasted_iota(jnp.int32, (rows, 128), 0)
+    lane = lax.broadcasted_iota(jnp.int32, (rows, 128), 1)
+    return jnp.sum(jnp.where(sub == lane, jnp.broadcast_to(row, (rows, 128)), 0), axis=1, keepdims=True)
+
+
+def destinations(wanted, n):
+    planes = n // LANES
+    sub = lax.broadcasted_iota(jnp.int32, (n, 128), 0) // LANES
+    lane = lax.broadcasted_iota(jnp.int32, (n, 128), 1)
+    hit = wanted == lane
+    top = jnp.max(jnp.where(hit, sub, -1), axis=0, keepdims=True)
+    low = jnp.min(jnp.where(hit, sub, planes), axis=0, keepdims=True)
+    return top, low
+
+
+def info_kernel(groups, n, owner_ref, slot_ref, spans_ref, request_ref, table_ref, mine, rows, send_sem, recv_sem):
+    planes = n // LANES
+    grp, me = lax.axis_index("grp"), lax.axis_index("req")
+    total = groups * n
+    flat = grp * n + me
+    barrier = pltpu.get_barrier_semaphore()
+
+    def other(k):
+        to = lax.rem(flat + k, total)
+        return lax.div(to, n), lax.rem(to, n)
+
+    for k in range(1, total):
+        pl.semaphore_signal(barrier, inc=1, device_id=other(k), device_id_type=MESH)
+    request = request_ref[0]
+    wanted = jnp.where(spans_ref[request] > 0, owner_ref[request], -1)
+    served = jnp.int32(0)
+    for r in range(n):
+        served = jnp.maximum(served, jnp.where(owner_ref[r] == me, slot_ref[r], 0))
+    mine[...] = jnp.full((1, 128), wanted, jnp.int32)
+    pl.semaphore_wait(barrier, total - 1)
+    copies = []
+    for k in range(1, total):
+        to_grp, to_req = other(k)
+        row = lax.rem(grp - to_grp + groups, groups) * n + me
+        copy = pltpu.make_async_remote_copy(
+            src_ref=mine, dst_ref=rows.at[row], send_sem=send_sem.at[k], recv_sem=recv_sem.at[k],
+            device_id=(to_grp, to_req), device_id_type=MESH,
+        )
+        copy.start()
+        copies.append(copy)
+    rows[pl.ds(me, 1)] = mine[...].reshape(1, 1, 128)
+    for copy in copies:
+        copy.wait()
+
+    need = jnp.zeros((1, 1), jnp.int32)
+    lane_row = lax.broadcasted_iota(jnp.int32, (1, 128), 1)
+    home = lane_row // LANES
+    for g in range(groups):
+        top, low = destinations(rows[g * n : (g + 1) * n].reshape(n, 128), n)
+        for cut in range(planes - 1):
+            up = jnp.sum(((home <= cut) & (top > cut) & (lane_row < n)).astype(jnp.int32), axis=1, keepdims=True)
+            down = jnp.sum(((home > cut) & (low <= cut) & (lane_row < n)).astype(jnp.int32), axis=1, keepdims=True)
+            need = jnp.maximum(need, jnp.maximum(up, down))
+
+    z = me // LANES
+    wants = rows[0:n].reshape(n, 128)
+    top, low = destinations(wants, n)
+    sub = lax.broadcasted_iota(jnp.int32, (n, 128), 0)
+    lane = lax.broadcasted_iota(jnp.int32, (n, 128), 1)
+    wants_row = jnp.sum(jnp.where(sub == lane, wants, 0), axis=0, keepdims=True)
+    col = lax.broadcasted_iota(jnp.int32, (n, 1), 0)
+    col_home = col // LANES
+    top_col, low_col = masked_column(top, n), masked_column(low, n)
+
+    def up_set(where_home, where_top, cut):
+        return (where_home <= cut) & (where_top > cut)
+
+    def down_set(where_home, where_low, cut):
+        return (where_home > cut) & (where_low <= cut)
+
+    def rank(inside, key_row, key_col):
+        ahead = inside & (key_row < key_col) & (lane_row < n)
+        return jnp.sum(ahead.astype(jnp.int32), axis=1, keepdims=True)
+
+    up_row, up_col = (planes - top) * n + lane_row, (planes - top_col) * n + col
+    down_row, down_col = (low + 1) * n + lane_row, (low_col + 1) * n + col
+    up_in = rank(up_set(home, top, z - 1), up_row, up_col)
+    up_out = rank(up_set(home, top, z), up_row, up_col)
+    down_in = rank(down_set(home, low, z), down_row, down_col)
+    down_out = rank(down_set(home, low, z - 1), down_row, down_col)
+    near = lax.rem(col, LANES)
+    src_up = jnp.where(col_home == z, near, LANES + up_in)
+    src_down = jnp.where(col_home == z, near, LANES + down_in)
+    src_fin = jnp.where(col_home == z, near, jnp.where(col_home < z, LANES + up_in, LANES + n + down_in))
+    sel_up = jnp.sum(jnp.where(up_set(col_home, top_col, z) & (up_out == lane), src_up, 0), axis=0, keepdims=True)
+    sel_down = jnp.sum(jnp.where(down_set(col_home, low_col, z - 1) & (down_out == lane), src_down, 0), axis=0, keepdims=True)
+    sel_fin = jnp.sum(jnp.where(wants_row == col, src_fin, 0), axis=0, keepdims=True)
+    sel_fin = jnp.where(wants_row < 0, -1, sel_fin)
+    table_ref[...] = jnp.zeros_like(table_ref)
+    table_ref[0:1, :] = sel_up
+    table_ref[1:2, :] = sel_down
+    table_ref[2:3, :] = sel_fin
+    table_ref[3:4, :] = jnp.broadcast_to(need, (1, 128))
+    table_ref[4:5, :] = jnp.full((1, 128), served, jnp.int32)
+
+
+def info(mesh, hit_owner, hit_slot, hit_spans, request_of):
+    groups, n = mesh.shape["grp"], mesh.shape["req"]
+    smem = pl.BlockSpec(memory_space=pltpu.SMEM)
+    return pl.pallas_call(
+        functools.partial(info_kernel, groups, n),
+        out_shape=jax.ShapeDtypeStruct((8, 128), jnp.int32),
+        in_specs=[smem] * 4,
+        out_specs=pl.BlockSpec(memory_space=pltpu.VMEM),
+        scratch_shapes=[
+            pltpu.VMEM((1, 128), jnp.int32),
+            pltpu.VMEM((groups * n, 1, 128), jnp.int32),
+            pltpu.SemaphoreType.DMA((groups * n,)),
+            pltpu.SemaphoreType.DMA((groups * n,)),
+        ],
+        compiler_params=pltpu.CompilerParams(collective_id=0, has_side_effects=True, vmem_limit_bytes=8 * 2**20),
+        name="info",
+    )(hit_owner, hit_slot, hit_spans, request_of)
+
+
+def route_kernel(
+    n, slots, tab, states_ref, tails_ref, start, tail_out,
+    three, own, own_tail, packed, plane, plane_t, up_recv, up_recv_t, down_recv, down_recv_t,
+    up_send, up_send_t, down_send, down_send_t, fin_send, fin_send_t,
+    load_sem, spread_s, spread_r, spread_ts, spread_tr, up_s, up_r, up_ts, up_tr,
+    down_s, down_r, down_ts, down_tr, fin_s, fin_r, fin_ts, fin_tr,
 ):
+    planes = n // LANES
+    steps = CHUNKS * slots
+    grp, me = lax.axis_index("grp"), lax.axis_index("req")
+    z, l = lax.div(me, LANES), lax.rem(me, LANES)
+    first, last = z == 0, z == planes - 1
+
+    def mate(k):
+        return z * LANES + lax.rem(l + k, LANES)
+
+    loads = []
+    for i in range(states_ref.shape[0]):
+        load = pltpu.make_async_copy(states_ref.at[i], three.at[i], load_sem.at[i])
+        load.start()
+        loads.append(load)
+    barrier = pltpu.get_barrier_semaphore()
+    for k in range(1, LANES):
+        pl.semaphore_signal(barrier, inc=1, device_id=(grp, mate(k)), device_id_type=MESH)
+
+    @pl.when(jnp.logical_not(first))
+    def _():
+        pl.semaphore_signal(barrier, inc=1, device_id=(grp, me - LANES), device_id_type=MESH)
+
+    @pl.when(jnp.logical_not(last))
+    def _():
+        pl.semaphore_signal(barrier, inc=1, device_id=(grp, me + LANES), device_id_type=MESH)
+
+    served = tab[4, 0]
+    tail = tails_ref[served].astype(jnp.float32)
+    packed[...] = jnp.zeros_like(packed)
+    for q in range(-(-tail.shape[1] // WIDE)):
+        for p in range(LANES):
+            at = q * WIDE + p * CC
+            if at < tail.shape[1]:
+                packed[p, 3 * q : 3 * q + 3, :] = tail[:, at : at + CC]
+    own_tail[...] = packed[...].astype(jnp.bfloat16)
+    for load in loads:
+        load.wait()
+
+    def take(c):
+        for p in range(LANES):
+            own[p, c] = three[served, :, p * WIDE + c * CC : p * WIDE + (c + 1) * CC]
+
+    for c in range(CHUNKS):
+        take(c)
+    for c in range(CHUNKS):
+        plane[c, pl.ds(l, 1)] = own[pl.ds(l, 1), c]
+    plane_t[pl.ds(l, 1)] = own_tail[pl.ds(l, 1)]
+
+    pl.semaphore_wait(barrier, LANES - 1 + jnp.where(first | last, 1, 2))
+
+    def remote(src, dst, ss, rs, to):
+        return pltpu.make_async_remote_copy(
+            src_ref=src, dst_ref=dst, send_sem=ss, recv_sem=rs, device_id=(grp, to), device_id_type=MESH
+        )
+
+    def spread(c, k):
+        to = lax.rem(l + k, LANES)
+        return remote(own.at[to, c], plane.at[c, l], spread_s.at[c, k - 1], spread_r.at[c, k - 1], mate(k))
+
+    def spread_tail(k):
+        to = lax.rem(l + k, LANES)
+        return remote(own_tail.at[to], plane_t.at[l], spread_ts.at[k - 1], spread_tr.at[k - 1], mate(k))
+
+    def spread_from(c, k):
+        frm = lax.rem(l + LANES - k, LANES)
+        return remote(own.at[frm, c], plane.at[c, frm], spread_s.at[c, k - 1], spread_r.at[c, k - 1], mate(k))
+
+    def spread_tail_from(k):
+        frm = lax.rem(l + LANES - k, LANES)
+        return remote(own_tail.at[frm], plane_t.at[frm], spread_ts.at[k - 1], spread_tr.at[k - 1], mate(k))
+
+    def up(s):
+        return remote(up_send.at[s], up_recv.at[s], up_s.at[s], up_r.at[s], me + LANES)
+
+    def up_tail(s):
+        return remote(up_send_t.at[s], up_recv_t.at[s], up_ts.at[s], up_tr.at[s], me + LANES)
+
+    def down(s):
+        return remote(down_send.at[s], down_recv.at[s], down_s.at[s], down_r.at[s], me - LANES)
+
+    def down_tail(s):
+        return remote(down_send_t.at[s], down_recv_t.at[s], down_ts.at[s], down_tr.at[s], me - LANES)
+
+    def fin(c, k):
+        to = lax.rem(l + k, LANES)
+        return remote(fin_send.at[c, k - 1], start.at[l, c], fin_s.at[c, k - 1], fin_r.at[c, k - 1], mate(k))
+
+    def fin_from(c, k):
+        frm = lax.rem(l + LANES - k, LANES)
+        return remote(fin_send.at[c, k - 1], start.at[frm, c], fin_s.at[c, k - 1], fin_r.at[c, k - 1], mate(k))
+
+    def fin_tail(k):
+        return remote(fin_send_t.at[k - 1], tail_out.at[l], fin_ts.at[k - 1], fin_tr.at[k - 1], mate(k))
+
+    def fin_tail_from(k):
+        frm = lax.rem(l + LANES - k, LANES)
+        return remote(fin_send_t.at[k - 1], tail_out.at[frm], fin_ts.at[k - 1], fin_tr.at[k - 1], mate(k))
+
+    for k in range(1, LANES):
+        spread_tail(k).start()
+    for c in range(min(2, CHUNKS)):
+        for k in range(1, LANES):
+            spread(c, k).start()
+
+    def fill(dst, at, sel, near, c, far, base, j, inner):
+        value = near[c, 0]
+        for p in range(1, LANES):
+            value = lax.select_n(sel == p, value, near[c, p])
+        dst[at] = value
+
+        @pl.when(inner)
+        def _():
+            def one(i, _):
+                dst[at] = lax.select_n(sel == LANES + i, dst[at], far[base + i])
+                return 0
+
+            lax.fori_loop(0, j + 1, one, 0)
+
+    def fill_tail(dst, j, sel, far, inner):
+        value = plane_t[0]
+        for p in range(1, LANES):
+            value = lax.select_n(sel == p, value, plane_t[p])
+        dst[j] = value
+
+        @pl.when(inner)
+        def _():
+            def one(i, _):
+                dst[j] = lax.select_n(sel == LANES + i, dst[j], far[i])
+                return 0
+
+            lax.fori_loop(0, j + 1, one, 0)
+
+    def tick(t, _):
+        tp = t - LAG * jnp.minimum(z, planes - 1 - z)
+
+        @pl.when((tp >= 0) & (tp < steps) & (lax.rem(jnp.maximum(tp, 0), slots) == 0))
+        def _():
+            c = lax.div(tp, slots)
+
+            @pl.when(c == 0)
+            def _():
+                for k in range(1, LANES):
+                    spread_tail_from(k).wait_recv()
+
+            for k in range(1, LANES):
+                spread_from(c, k).wait_recv()
+
+            @pl.when(c + 2 < CHUNKS)
+            def _():
+                for k in range(1, LANES):
+                    spread(c + 2, k).start()
+
+        def along(s, row, edge_in, edge_out, copy, copy_tail, send, send_t, recv, recv_t):
+            @pl.when((s >= 0) & (s < steps))
+            def _():
+                c, j = lax.div(s, slots), lax.rem(s, slots)
+                inner = jnp.logical_not(edge_in)
+
+                @pl.when(inner)
+                def _():
+                    @pl.when(c == 0)
+                    def _():
+                        copy_tail(j).wait_recv()
+
+                    copy(s).wait_recv()
+
+                @pl.when(jnp.logical_not(edge_out))
+                def _():
+                    sel = tab[row, j]
+
+                    @pl.when(c == 0)
+                    def _():
+                        fill_tail(send_t, j, sel, recv_t, inner)
+                        copy_tail(j).start()
+
+                    fill(send, s, sel, plane, c, recv, c * slots, j, inner)
+
+                    @pl.when(s >= 2)
+                    def _():
+                        copy(s - 2).wait_send()
+
+                    copy(s).start()
+
+        along(t - LAG * z, 0, first, last, up, up_tail, up_send, up_send_t, up_recv, up_recv_t)
+        along(t - LAG * (planes - 1 - z), 1, last, first, down, down_tail, down_send, down_send_t, down_recv, down_recv_t)
+
+        tf = t - LAG * jnp.maximum(z, planes - 1 - z)
+
+        @pl.when((tf >= 0) & (tf < steps) & (lax.rem(jnp.maximum(tf, 0), slots) == slots - 1))
+        def _():
+            c = lax.div(tf, slots)
+            sels = [tab[2, mate(k)] for k in range(LANES)]
+
+            def choose(near, far_up, far_down, write, read):
+                acc = [jnp.zeros(near(0).shape, jnp.bfloat16)] * LANES
+                for p in range(LANES):
+                    value = near(p)
+                    acc = [lax.select_n(sel == p, a, value) for sel, a in zip(sels, acc)]
+                for k in range(LANES):
+                    write(k, acc[k])
+
+                def far(get, base):
+                    acc = [read(k) for k in range(LANES)]
+                    for i in range(slots):
+                        value = get(i)
+                        acc = [lax.select_n(sel == base + i, a, value) for sel, a in zip(sels, acc)]
+                    for k in range(LANES):
+                        write(k, acc[k])
+
+                @pl.when(jnp.logical_not(first))
+                def _():
+                    far(far_up, LANES)
+
+                @pl.when(jnp.logical_not(last))
+                def _():
+                    far(far_down, LANES + n)
+
+            def rows_of(b, _):
+                at = pl.ds(pl.multiple_of(b * 16, 16), 16)
+
+                def write(k, v):
+                    if k == 0:
+                        start[l, c, at] = v
+                    else:
+                        fin_send[c, k - 1, at] = v
+
+                def read(k):
+                    return start[l, c, at] if k == 0 else fin_send[c, k - 1, at]
+
+                choose(lambda p: plane[c, p, at], lambda i: up_recv[c * slots + i, at],
+                       lambda i: down_recv[c * slots + i, at], write, read)
+                return 0
+
+            lax.fori_loop(0, NST // 16, rows_of, 0)
+            for k in range(1, LANES):
+                fin(c, k).start()
+
+            @pl.when(c == 0)
+            def _():
+                def write(k, v):
+                    if k == 0:
+                        tail_out[l] = v
+                    else:
+                        fin_send_t[k - 1] = v
+
+                def read(k):
+                    return tail_out[l] if k == 0 else fin_send_t[k - 1]
+
+                choose(lambda p: plane_t[p], lambda i: up_recv_t[i], lambda i: down_recv_t[i], write, read)
+                for k in range(1, LANES):
+                    fin_tail(k).start()
+
+        return 0
+
+    lax.fori_loop(0, steps + LAG * (planes - 1), tick, 0)
+
+    for k in range(1, LANES):
+        spread_tail(k).wait_send()
+        fin_tail(k).wait_send()
+        fin_tail_from(k).wait_recv()
+        for c in range(CHUNKS):
+            spread(c, k).wait_send()
+            fin(c, k).wait_send()
+            fin_from(c, k).wait_recv()
+
+    @pl.when(jnp.logical_not(last))
+    def _():
+        for j in range(slots):
+            up_tail(j).wait_send()
+        for s in range(max(steps - 2, 0), steps):
+            up(s).wait_send()
+
+    @pl.when(jnp.logical_not(first))
+    def _():
+        for j in range(slots):
+            down_tail(j).wait_send()
+        for s in range(max(steps - 2, 0), steps):
+            down(s).wait_send()
+
+
+def route(n, slots, number, table, cache_states, cache_tails):
+    steps = CHUNKS * slots
+    big = lambda *lead: pltpu.VMEM(lead + (NST, CC), jnp.bfloat16)
+    small = lambda *lead: pltpu.VMEM(lead + (TAIL_ROWS, CC), jnp.bfloat16)
+    sem = lambda *shape: [pltpu.SemaphoreType.DMA(shape)] * 2
+    vmem = pl.BlockSpec(memory_space=pltpu.VMEM)
+    return pl.pallas_call(
+        functools.partial(route_kernel, n, slots),
+        out_shape=(
+            jax.ShapeDtypeStruct((LANES, CHUNKS, NST, CC), jnp.bfloat16),
+            jax.ShapeDtypeStruct((LANES, TAIL_ROWS, CC), jnp.bfloat16),
+        ),
+        in_specs=[pl.BlockSpec(memory_space=pltpu.SMEM), pl.BlockSpec(memory_space=pl.ANY), vmem],
+        out_specs=(vmem, vmem),
+        scratch_shapes=[
+            pltpu.VMEM(cache_states.shape, jnp.bfloat16),
+            big(LANES, CHUNKS), small(LANES), pltpu.VMEM((LANES, TAIL_ROWS, CC), jnp.float32),
+            big(CHUNKS, LANES), small(LANES),
+            big(steps), small(slots), big(steps), small(slots),
+            big(steps), small(slots), big(steps), small(slots),
+            big(CHUNKS, LANES - 1), small(LANES - 1),
+            pltpu.SemaphoreType.DMA((cache_states.shape[0],)),
+            *sem(CHUNKS, LANES - 1), *sem(LANES - 1),
+            *sem(steps), *sem(slots), *sem(steps), *sem(slots),
+            *sem(CHUNKS, LANES - 1), *sem(LANES - 1),
+        ],
+        compiler_params=pltpu.CompilerParams(
+            collective_id=number, has_side_effects=True, vmem_limit_bytes=48 * 2**20
+        ),
+        name=f"route{slots}",
+    )(table, cache_states, cache_tails)
+
+
+def fetch(mesh, cache_states, cache_tails, hit_owner, hit_slot, hit_spans, request_of):
+    n = mesh.shape["req"]
+    table = info(mesh, hit_owner, hit_slot, hit_spans, request_of)
+    need = table[3, 0]
+    sizes = [3, 4, n // 2]
+    which = sum((need > size).astype(jnp.int32) for size in sizes[:-1])
+    start, tail = lax.switch(
+        which,
+        [functools.partial(route, n, size, 1 + i) for i, size in enumerate(sizes)],
+        table, cache_states, cache_tails,
+    )
+    tail = tail.transpose(1, 0, 2).reshape(TAIL_ROWS, WIDE)[:15].reshape(5, 3, WIDE)
+    tail = tail.transpose(1, 0, 2).reshape(3, 5 * WIDE)[:, : cache_tails.shape[2]]
+    return start, tail
+
+
+def fetch_any(cache_states, cache_tails, hit_owner, hit_slot, hit_spans, request_of):
     count = hit_owner.shape[0]
-    rows = xbc.shape[0]
     mine = request_of[0]
     live = (hit_spans[mine] > 0).astype(jnp.int32)
     device = lax.axis_index("req")
@@ -127,10 +595,22 @@
     )
     chosen = pick(parts, owners)
     start = lax.all_to_all(chosen, "req", split_axis=0, concat_axis=0, tiled=True).reshape(NST, INNER)
-
+    start = jnp.where(live > 0, start, jnp.zeros_like(start))
+    start = start.reshape(NST, LANES, CHUNKS, CC).transpose(1, 2, 0, 3)
     tail = lax.dynamic_index_in_dim(every_tail, hit_owner[mine], 0, keepdims=False)
-    tail = jnp.where(live > 0, tail, jnp.zeros_like(tail)).astype(jnp.float32)
-    tail = jnp.pad(tail, ((5, 0), (0, 0)))
+    return start, jnp.where(live > 0, tail, jnp.zeros_like(tail))
+
+
+def local(
+    mesh, xbc, dt_raw, conv_weight, conv_bias, dt_bias, a_log, d_skip, cache_states, cache_tails,
+    hit_owner, hit_slot, hit_spans, request_of,
+):
+    rows = xbc.shape[0]
+    if mesh.shape["req"] == 16:
+        start, tail = fetch(mesh, cache_states, cache_tails, hit_owner, hit_slot, hit_spans, request_of)
+    else:
+        start, tail = fetch_any(cache_states, cache_tails, hit_owner, hit_slot, hit_spans, request_of)
+    tail = jnp.pad(tail.astype(jnp.float32), ((5, 0), (0, 0)))
     step = jax.nn.softplus(dt_raw + dt_bias[None, :])
     below = jnp.tril(jnp.ones((rows, rows), jnp.float32))
     cum = jnp.dot(below, step * (-jnp.exp(a_log))[None, :], precision=lax.Precision.HIGHEST)
@@ -177,11 +657,14 @@
             jax.ShapeDtypeStruct((rows, INNER), jnp.bfloat16),
             jax.ShapeDtypeStruct((1, NST, INNER), jnp.bfloat16),
         ),
-        in_specs=[pl.BlockSpec(memory_space=pltpu.SMEM), wide(NST), wide(rows), wide(NST), group, tall, wide(1)],
+        in_specs=[
+            pl.BlockSpec((1, COLS // CC, NST, CC), lambda i: (i // 2, i % 2, 0, 0)),
+            wide(rows), wide(NST), group, tall, wide(1),
+        ],
         out_specs=(wide(rows), pl.BlockSpec((1, NST, COLS), lambda i: (0, 0, i))),
         compiler_params=pltpu.CompilerParams(vmem_limit_bytes=58 * 2**20),
         name="state",
-    )(live[None], start, y_local, fresh, c_part, by_step(jnp.exp(cum)), elast)
+    )(start, y_local, fresh, c_part, by_step(jnp.exp(cum)), elast)
 
 
 def solution(mesh):
@@ -190,4 +673,4 @@
     in_specs = (
         rows, rows, P(), P(), P(), P(), P(), slots, slots, P("grp"), P("grp"), P("grp"), P(("grp", "req")),
     )
-    return jax.shard_map(local, mesh=mesh, in_specs=in_specs, out_specs=(rows, slots), check_vma=False)
+    return jax.shard_map(functools.partial(local, mesh), mesh=mesh, in_specs=in_specs, out_specs=(rows, slots), check_vma=False)

time: 151 us -> 114 us (0.75)
  the two profiles are of different devices: /device:TPU:15 before, /device:TPU:1 now
where the time goes in v1:
time: 114 us
  Pallas kernels  98.6 us (86%)
  local copies, waits for them, and re-layouts  9.03 us (8%)
  other arithmetic  2.98 us (3%)
  between operations  2.69 us (2%)
    pallas_call x1, Pallas kernels, route(): pl.pallas_call(functools.partial(route_kernel, n, slots), out_shape=(jax....  66.7 us
    pallas_call x1, Pallas kernels, local(): pl.pallas_call(local_kernel, grid=(STEPS,), out_shape=(jax.ShapeDtypeStru...  13.3 us
    pallas_call x1, Pallas kernels, info(): pl.pallas_call(functools.partial(info_kernel, groups, n), out_shape=jax.S...  10.1 us
    pallas_call x1, Pallas kernels, local(): pl.pallas_call(state_kernel, grid=(STEPS,), out_shape=(jax.ShapeDtypeStru...  8.55 us
    reshape x3, local copies, waits for them, and re-layouts, by_step(): return a.reshape(a.shape[0], STEPS, PER_STEP).transpose(1, 0, 2)  3.04 us
    unnamed x13, local copies, waits for them, and re-layouts  2.91 us

profile of v1, /device:TPU:1, one launch (start us, length us, event | category | flops | bytes accessed | tf_op | source)
XLA Modules:
  0.0 113.6 jit_solution(17051452721791086511)
XLA Ops:
  1.3 0.7 exponential_negate_fusion
  1.9 0.0 copy-start
  1.9 0.7 copy-done
  2.6 0.0 copy-start.1
  2.6 0.7 copy-done.1
  3.3 0.0 copy-start.2
  3.3 0.7 copy-done.2
  3.9 0.0 copy-start.3
  3.9 10.1 %info.1 = s32[8,128]{1,0:T(8,128)S(1)} custom-call(s32[16]{0:T(128)S(1)} %copy-done, s32[16]{0:T(128)S(1)} %copy-done.1, s32[16]{0:T(128)S(1)} %copy-done.2, s32[1]{0:T(128)S(6)} %copy.27.request_ref), custom_call_target="tpu_custom_call" | custom-call | tf_op jit(solution)/shard_map/info/pallas_call | solution.py:226
  14.0 0.5 slice.13
  15.8 0.9 copy.17
  16.8 0.8 compare_select_fusion
  17.6 0.0 copy-start.5
  17.6 0.3 fusion
  17.8 0.0 copy-start.4
  17.8 0.2 slice_reduce_fusion
  18.0 0.1 broadcast_in_dim.22
  18.1 0.7 broadcast_in_dim_reshape.7.elast_ref
  18.8 0.8 fusion.8
  19.6 0.7 broadcast_in_dim.21
  20.4 0.7 broadcast_in_dim_reshape.6.skip_ref
  21.1 1.0 copy.19
  22.1 1.0 copy.20
  23.1 1.0 copy.18
  24.1 0.0 copy-done.3
  24.1 0.0 copy-done.5
  24.1 0.0 copy-done.4
  24.1 66.7 %conditional.1 = ((bf16[4,4,128,512]{3,2,1,0:T(8,128)(2,1)S(1)}, bf16[4,16,512]{2,1,0:T(8,128)(2,1)S(1)})) conditional(s32[]{:T(128)} %bitcast, (s32[8,128]{1,0:T(8,128)S(1)}, bf16[3,128,8192]{2,1,0:T(8,128)(2,1)}, bf16[3,3,9216]{2,1,0:T(4,128)(2,1)S(1)}) %tuple.24, (s32[8,128]{1,0:T(8,128)S(1)}, bf16[3,128,8192]{2,1,0:T(8,128)(2,1)}, ...), branch_computations={%region_0.0_spmd, %region_1.0_spmd, %region_2.0_spmd} | conditional | bytes 8 | solution.py:568
  24.1 66.7 %route3.1 = (bf16[4,4,128,512]{3,2,1,0:T(8,128)(2,1)S(1)}, bf16[4,16,512]{2,1,0:T(8,128)(2,1)S(1)}) custom-call(s32[8,128]{1,0:T(8,128)S(1)} %get-tuple-element.18.tab, bf16[3,128,8192]{2,1,0:T(8,128)(2,1)} %get-tuple-element.19.states_ref, bf16[3,3,9216]{2,1,0:T(4,128)(2,1)S(1)} %get-tuple-element.20.tails_ref), custom_call_target="tpu_custom_call" | custom-call | tf_op jit(solution)/shard_map/cond/branch_0_fun/route3/pallas_call | solution.py:535
  90.8 0.1 copy.16
  91.0 0.8 pad_convert_fusion.tx_ref.tb_ref.tc_ref
  91.8 13.3 %local.1 = (f32[128,8192]{1,0:T(8,128)}, f32[128,8192]{1,0:T(8,128)}, bf16[128,512]{1,0:T(8,128)(2,1)}) custom-call(bf16[128,9216]{1,0:T(8,128)(2,1)} %xc_ref.1, bf16[128,9216]{1,0:T(8,128)(2,1)} %xc_ref.1, bf16[128,9216]{1,0:T(8,128)(2,1)} %xc_ref.1, f32[8,9216]{1,0:T(8,128)} %pad_convert_fusion.tx_ref.tb_ref.tc_ref, ...), custom_call_target="tpu_custom_call" | custom-call | flops 1000000000 | bytes 40000000 | tf_op jit(solution)/shard_map/local/pallas_call | solution.py:636
  105.1 8.5 %state.1 = (bf16[128,8192]{1,0:T(8,128)(2,1)}, bf16[1,128,8192]{2,1,0:T(8,128)(2,1)}) custom-call(bf16[4,4,128,512]{3,2,1,0:T(8,128)(2,1)S(1)} %get-tuple-element.34.start_ref, f32[128,8192]{1,0:T(8,128)} %get-tuple-element.36.y_ref, f32[128,8192]{1,0:T(8,128)} %get-tuple-element.37.fresh_ref, bf16[128,512]{1,0:T(8,128)(2,1)} %get-tuple-element.38.c_ref, ...), custom_call_target="tpu_custom_call" | custom-call | tf_op jit(solution)/shard_map/state/pallas_call | solution.py:653
  (3 shorter events, 0.1 us)
Async XLA Ops:
  1.9 0.7 copy-start
  2.6 0.7 copy-start.1
  3.3 0.7 copy-start.2
  3.9 20.2 %copy-start.3 = (bf16[3,3,9216]{2,1,0:T(4,128)(2,1)S(1)}, bf16[3,3,9216]{2,1,0:T(4,128)(2,1)}, u32[]{:S(2)}) copy-start(bf16[3,3,9216]{2,1,0:T(4,128)(2,1)} %param.24) | copy-start | bytes 497668
  17.6 6.6 %copy-start.5 = (f32[128,128]{0,1:T(8,128)}, f32[128,128]{0,1:T(8,128)S(1)}, u32[]{:S(2)}) copy-start(f32[128,128]{0,1:T(8,128)S(1)} %compare_select_fusion) | copy-start | bytes 196612
  17.8 6.3 %copy-start.4 = (f32[128,128]{0,1:T(8,128)}, f32[128,128]{0,1:T(8,128)S(1)}, u32[]{:S(2)}) copy-start(f32[128,128]{0,1:T(8,128)S(1)} %fusion) | copy-start | bytes 196612

commit v2 on v1

--- a/solution.py
+++ b/solution.py
@@ -87,22 +87,18 @@
     )
 
 
-def state_kernel(start_ref, y_ref, fresh_ref, c_ref, ecum_ref, elast_ref, y_out_ref, final_ref):
+def state_kernel(live_ref, start_ref, y_ref, fresh_ref, c_ref, ecum_ref, elast_ref, y_out_ref, final_ref):
     rows = y_ref.shape[0]
+    start = start_ref[...]
+    start = jnp.where(live_ref[0] > 0, start, jnp.zeros_like(start))
     low = lax.broadcasted_iota(jnp.int32, (rows, 128), 1) < HEAD_DIM
     ecum = ecum_ref[0]
-    for half in range(COLS // CC):
-        start = start_ref[0, half]
-        here = slice(half * CC, (half + 1) * CC)
-        ys = jnp.dot(c_ref[...], start, preferred_element_type=jnp.float32)
-        for j in range(half * CC // HEAD_DIM, (half + 1) * CC // HEAD_DIM, 2):
-            sl = slice(j * HEAD_DIM, (j + 2) * HEAD_DIM)
-            factor = jnp.where(low, ecum[:, j : j + 1], ecum[:, j + 1 : j + 2])
-            inner = slice(j * HEAD_DIM - half * CC, (j + 2) * HEAD_DIM - half * CC)
-            y_out_ref[:, sl] = (y_ref[:, sl] + factor * ys[:, inner]).astype(jnp.bfloat16)
-        final_ref[0, :, here] = (
-            elast_ref[:, here] * start.astype(jnp.float32) + fresh_ref[:, here]
-        ).astype(jnp.bfloat16)
+    ys = jnp.dot(c_ref[...], start, preferred_element_type=jnp.float32)
+    for j in range(0, PER_STEP, 2):
+        sl = slice(j * HEAD_DIM, (j + 2) * HEAD_DIM)
+        factor = jnp.where(low, ecum[:, j : j + 1], ecum[:, j + 1 : j + 2])
+        y_out_ref[:, sl] = (y_ref[:, sl] + factor * ys[:, sl]).astype(jnp.bfloat16)
+    final_ref[0] = (elast_ref[...] * start.astype(jnp.float32) + fresh_ref[...]).astype(jnp.bfloat16)
 
 
 def by_step(a):
@@ -239,8 +235,18 @@
     )(hit_owner, hit_slot, hit_spans, request_of)
 
 
+def conv(taps, bias, pad, rows):
+    v = jnp.broadcast_to(bias, (rows, bias.shape[1]))
+    for k in range(4):
+        v = v + taps[k : k + 1, :] * pad[5 + k : 5 + k + rows, :]
+    return (v / (1.0 + jnp.exp(-v))).astype(jnp.bfloat16)
+
+
 def route_kernel(
-    n, slots, tab, states_ref, tails_ref, start, tail_out,
+    n, slots, tab, states_ref, tails_ref, xbc_ref, dt_ref, weight_ref, bias_ref, dt_bias_ref, a_log_ref, skip_ref,
+    y_out, final_out,
+    start, tail_out, xs, pad, head_pad, tail_rows, cum_ref, cumt_ref, stept_ref, coef_ref, ecum_ref, elast_ref,
+    scores_ref, y_local, fresh, y_stage, f_stage, y_sem, f_sem,
     three, own, own_tail, packed, plane, plane_t, up_recv, up_recv_t, down_recv, down_recv_t,
     up_send, up_send_t, down_send, down_send_t, fin_send, fin_send_t,
     load_sem, spread_s, spread_r, spread_ts, spread_tr, up_s, up_r, up_ts, up_tr,
@@ -350,6 +356,168 @@
         for k in range(1, LANES):
             spread(c, k).start()
 
+    rows = xbc_ref.shape[0]
+    channels = xbc_ref.shape[1]
+    pieces = channels // CC
+    heads = CC // HEAD_DIM
+    first_b, first_c = INNER, INNER + GROUPS * NST
+    low = lax.broadcasted_iota(jnp.int32, (rows, 128), 1) < HEAD_DIM
+    low_n = lax.broadcasted_iota(jnp.int32, (NST, 128), 1) < HEAD_DIM
+
+    def columns(i):
+        return pl.ds(pl.multiple_of(i * CC, CC), CC)
+
+    def head_terms():
+        step = jax.nn.softplus(dt_ref[...] + dt_bias_ref[...])
+        below = (
+            lax.broadcasted_iota(jnp.int32, (rows, rows), 0) >= lax.broadcasted_iota(jnp.int32, (rows, rows), 1)
+        ).astype(jnp.float32)
+        cum = jnp.dot(below, step * (-jnp.exp(a_log_ref[...])), precision=lax.Precision.HIGHEST,
+                      preferred_element_type=jnp.float32)
+        last = cum[rows - 1 : rows, :]
+        cum_ref[...] = cum
+        cumt_ref[...] = cum.T
+        stept_ref[...] = step.T
+        coef_ref[...] = jnp.exp(last - cum) * step
+        ecum_ref[...] = jnp.exp(cum)
+        elast_ref[...] = jnp.broadcast_to(jnp.exp(last), elast_ref.shape)
+
+    def conv_piece(i):
+        at = columns(i)
+        pad[0:8, :] = jnp.zeros((8, CC), jnp.float32)
+        pad[8 : 8 + rows, :] = xbc_ref[:, at].astype(jnp.float32)
+        xs[:, at] = conv(weight_ref[:, at], bias_ref[:, at], pad, rows)
+
+    def head_piece(i, _):
+        at = columns(i)
+        head_pad[0:8, :] = tail_rows[:, at]
+        head_pad[8:24, :] = xbc_ref[0:16, at].astype(jnp.float32)
+        xs[0:16, at] = conv(weight_ref[:, at], bias_ref[:, at], head_pad, 16)
+        return 0
+
+    def with_tail():
+        tail_rows[...] = jnp.zeros_like(tail_rows)
+        for p in range(LANES):
+            got = tail_out[p].astype(jnp.float32)
+            for q in range(-(-channels // WIDE)):
+                at = q * WIDE + p * CC
+                if at < channels:
+                    tail_rows[5:8, at : at + CC] = got[3 * q : 3 * q + 3, :]
+        lax.fori_loop(0, pieces, head_piece, 0)
+        causal = lax.broadcasted_iota(jnp.int32, (rows, rows), 0) >= lax.broadcasted_iota(jnp.int32, (rows, rows), 1)
+        for g in range(GROUPS):
+            b = xs[:, first_b + g * NST : first_b + (g + 1) * NST]
+            c = xs[:, first_c + g * NST : first_c + (g + 1) * NST]
+            scores = lax.dot_general(c, b, (((1,), (1,)), ((), ())), preferred_element_type=jnp.float32)
+            scores_ref[g] = jnp.where(causal, scores, 0.0)
+
+    def turned(ref, i):
+        return pltpu.roll(ref[...], lax.rem(128 - heads * i, 128), axis=1)
+
+    def scan_piece(p, c):
+        i = p * CHUNKS + c
+        at = columns(i)
+        x = xs[:, at]
+        scores = scores_ref[p]
+        cum, coef, skip = turned(cum_ref, i), turned(coef_ref, i), turned(skip_ref, i)
+        here = pl.ds(pl.multiple_of(i * heads, heads), heads)
+        cumt, stept = cumt_ref[here, :], stept_ref[here, :]
+        zero = jnp.zeros((rows, 128), jnp.bfloat16)
+        ys, carried = [], []
+        for j in range(0, heads, 2):
+            xp = x[:, j * HEAD_DIM : (j + 2) * HEAD_DIM]
+            mixes = []
+            for h in (j, j + 1):
+                decay = jnp.exp(jnp.minimum(cum[:, h : h + 1] - cumt[h : h + 1, :], 0.0))
+                mixes.append((scores * decay * stept[h : h + 1, :]).astype(jnp.bfloat16))
+            mix = jnp.concatenate(mixes, axis=1)
+            both = jnp.concatenate([jnp.where(low, xp, zero), jnp.where(low, zero, xp)], axis=0)
+            xf = xp.astype(jnp.float32)
+            d = jnp.where(low[0:1], skip[0:1, j : j + 1], skip[0:1, j + 1 : j + 2])
+            ys.append(jnp.dot(mix, both, preferred_element_type=jnp.float32) + d * xf)
+            carried.append((jnp.where(low, coef[:, j : j + 1], coef[:, j + 1 : j + 2]) * xf).astype(jnp.bfloat16))
+        y_local[i] = jnp.concatenate(ys, axis=1)
+        b = xs[:, pl.ds(pl.multiple_of(first_b + p * NST, NST), NST)]
+        fresh[i] = lax.dot_general(
+            b, jnp.concatenate(carried, axis=1), (((0,), (0,)), ((), ())), preferred_element_type=jnp.float32
+        )
+
+    def outputs(i):
+        return (
+            pltpu.make_async_copy(y_stage.at[i], y_out.at[:, columns(i)], y_sem.at[i]),
+            pltpu.make_async_copy(f_stage.at[i], final_out.at[0, :, columns(i)], f_sem.at[i]),
+        )
+
+    def last_piece(p, c):
+        i = p * CHUNKS + c
+        held = start[p, c]
+        ys = jnp.dot(xs[:, pl.ds(pl.multiple_of(first_c + p * NST, NST), NST)], held,
+                     preferred_element_type=jnp.float32)
+        ecum, elast = turned(ecum_ref, i), turned(elast_ref, i)
+        for j in range(0, heads, 2):
+            sl = slice(j * HEAD_DIM, (j + 2) * HEAD_DIM)
+            factor = jnp.where(low, ecum[:, j : j + 1], ecum[:, j + 1 : j + 2])
+            y_stage[i, :, sl] = (y_local[i, :, sl] + factor * ys[:, sl]).astype(jnp.bfloat16)
+            kept = jnp.where(low_n[0:1], elast[0:1, j : j + 1], elast[0:1, j + 1 : j + 2])
+            f_stage[i, :, sl] = (kept * held[:, sl].astype(jnp.float32) + fresh[i, :, sl]).astype(jnp.bfloat16)
+        for copy in outputs(i):
+            copy.start()
+
+    def last_chunk(c):
+        for k in range(1, LANES):
+            fin_from(c, k).wait_recv()
+
+        def one(p, _):
+            last_piece(p, c)
+            return 0
+
+        lax.fori_loop(0, LANES, one, 0)
+
+    ready = slots + LAG * (planes - 1)
+    total = steps + LAG * (planes - 1)
+    per_conv = -(-pieces // ready)
+    per_scan = -(-(LANES * CHUNKS) // (total - ready - 1))
+
+    lead = -(-LANES // per_scan)
+
+    def compute(t):
+        @pl.when(t < ready)
+        def _():
+            def one(u, _):
+                i = t * per_conv + u
+
+                @pl.when(i < pieces)
+                def _():
+                    conv_piece(i)
+
+                return 0
+
+            lax.fori_loop(0, per_conv, one, 0)
+
+        @pl.when(t == ready)
+        def _():
+            for k in range(1, LANES):
+                fin_tail_from(k).wait_recv()
+            with_tail()
+
+        @pl.when(t > ready)
+        def _():
+            def one(u, _):
+                i = (t - ready - 1) * per_scan + u
+
+                @pl.when(i < LANES * CHUNKS)
+                def _():
+                    scan_piece(lax.rem(i, LANES), lax.div(i, LANES))
+
+                return 0
+
+            lax.fori_loop(0, per_scan, one, 0)
+            since = t - ready - lead
+
+            @pl.when((since >= 0) & (lax.rem(jnp.maximum(since, 0), slots) == 0))
+            def _():
+                last_chunk(lax.div(since, slots))
+
     def fill(dst, at, sel, near, c, far, base, j, inner):
         value = near[c, 0]
         for p in range(1, LANES):
@@ -498,18 +666,20 @@
                 for k in range(1, LANES):
                     fin_tail(k).start()
 
+        compute(t)
         return 0
 
-    lax.fori_loop(0, steps + LAG * (planes - 1), tick, 0)
+    head_terms()
+    lax.fori_loop(0, total, tick, 0)
+    for c in range((total - 1 - ready - lead) // slots + 1, CHUNKS):
+        last_chunk(c)
 
     for k in range(1, LANES):
         spread_tail(k).wait_send()
         fin_tail(k).wait_send()
-        fin_tail_from(k).wait_recv()
         for c in range(CHUNKS):
             spread(c, k).wait_send()
             fin(c, k).wait_send()
-            fin_from(c, k).wait_recv()
 
     @pl.when(jnp.logical_not(last))
     def _():
@@ -525,24 +695,37 @@
         for s in range(max(steps - 2, 0), steps):
             down(s).wait_send()
 
-
-def route(n, slots, number, table, cache_states, cache_tails):
+    for i in range(LANES * CHUNKS):
+        for copy in outputs(i):
+            copy.wait()
+
+
+def route(n, slots, number, table, cache_states, cache_tails, xbc, dt_raw, weight, bias, dt_bias, a_log, skip):
     steps = CHUNKS * slots
+    rows, channels = xbc.shape
+    pieces = LANES * CHUNKS
+    f32 = lambda *shape: pltpu.VMEM(shape, jnp.float32)
     big = lambda *lead: pltpu.VMEM(lead + (NST, CC), jnp.bfloat16)
     small = lambda *lead: pltpu.VMEM(lead + (TAIL_ROWS, CC), jnp.bfloat16)
     sem = lambda *shape: [pltpu.SemaphoreType.DMA(shape)] * 2
     vmem = pl.BlockSpec(memory_space=pltpu.VMEM)
+    hbm = pl.BlockSpec(memory_space=pl.ANY)
     return pl.pallas_call(
         functools.partial(route_kernel, n, slots),
         out_shape=(
-            jax.ShapeDtypeStruct((LANES, CHUNKS, NST, CC), jnp.bfloat16),
-            jax.ShapeDtypeStruct((LANES, TAIL_ROWS, CC), jnp.bfloat16),
+            jax.ShapeDtypeStruct((rows, INNER), jnp.bfloat16),
+            jax.ShapeDtypeStruct((1, NST, INNER), jnp.bfloat16),
         ),
-        in_specs=[pl.BlockSpec(memory_space=pltpu.SMEM), pl.BlockSpec(memory_space=pl.ANY), vmem],
-        out_specs=(vmem, vmem),
+        in_specs=[pl.BlockSpec(memory_space=pltpu.SMEM), hbm] + [vmem] * 8,
+        out_specs=(hbm, hbm),
         scratch_shapes=[
+            big(LANES, CHUNKS), small(LANES),
+            pltpu.VMEM((rows, channels), jnp.bfloat16), f32(8 + rows, CC), f32(24, CC), f32(8, channels),
+            f32(rows, HEADS), f32(HEADS, rows), f32(HEADS, rows), f32(rows, HEADS), f32(rows, HEADS), f32(8, HEADS),
+            f32(GROUPS, rows, rows), f32(pieces, rows, CC), f32(pieces, NST, CC),
+            pltpu.VMEM((pieces, rows, CC), jnp.bfloat16), big(pieces), *sem(pieces),
             pltpu.VMEM(cache_states.shape, jnp.bfloat16),
-            big(LANES, CHUNKS), small(LANES), pltpu.VMEM((LANES, TAIL_ROWS, CC), jnp.float32),
+            big(LANES, CHUNKS), small(LANES), f32(LANES, TAIL_ROWS, CC),
             big(CHUNKS, LANES), small(LANES),
             big(steps), small(slots), big(steps), small(slots),
             big(steps), small(slots), big(steps), small(slots),
@@ -553,30 +736,35 @@
             *sem(CHUNKS, LANES - 1), *sem(LANES - 1),
         ],
         compiler_params=pltpu.CompilerParams(
-            collective_id=number, has_side_effects=True, vmem_limit_bytes=48 * 2**20
+            collective_id=number, has_side_effects=True, vmem_limit_bytes=58 * 2**20
         ),
         name=f"route{slots}",
-    )(table, cache_states, cache_tails)
-
-
-def fetch(mesh, cache_states, cache_tails, hit_owner, hit_slot, hit_spans, request_of):
+    )(table, cache_states, cache_tails, xbc, dt_raw, weight, bias, dt_bias, a_log, skip)
+
+
+def local_routed(
+    mesh, xbc, dt_raw, conv_weight, conv_bias, dt_bias, a_log, d_skip, cache_states, cache_tails,
+    hit_owner, hit_slot, hit_spans, request_of,
+):
     n = mesh.shape["req"]
     table = info(mesh, hit_owner, hit_slot, hit_spans, request_of)
     need = table[3, 0]
     sizes = [3, 4, n // 2]
     which = sum((need > size).astype(jnp.int32) for size in sizes[:-1])
-    start, tail = lax.switch(
+    return lax.switch(
         which,
         [functools.partial(route, n, size, 1 + i) for i, size in enumerate(sizes)],
-        table, cache_states, cache_tails,
+        table, cache_states, cache_tails, xbc, dt_raw, conv_weight, conv_bias[None], dt_bias[None], a_log[None],
+        jnp.broadcast_to(d_skip[None], (8, HEADS)),
     )
-    tail = tail.transpose(1, 0, 2).reshape(TAIL_ROWS, WIDE)[:15].reshape(5, 3, WIDE)
-    tail = tail.transpose(1, 0, 2).reshape(3, 5 * WIDE)[:, : cache_tails.shape[2]]
-    return start, tail
-
-
-def fetch_any(cache_states, cache_tails, hit_owner, hit_slot, hit_spans, request_of):
+
+
+def local(
+    xbc, dt_raw, conv_weight, conv_bias, dt_bias, a_log, d_skip, cache_states, cache_tails,
+    hit_owner, hit_slot, hit_spans, request_of,
+):
     count = hit_owner.shape[0]
+    rows = xbc.shape[0]
     mine = request_of[0]
     live = (hit_spans[mine] > 0).astype(jnp.int32)
     device = lax.axis_index("req")
@@ -595,22 +783,10 @@
     )
     chosen = pick(parts, owners)
     start = lax.all_to_all(chosen, "req", split_axis=0, concat_axis=0, tiled=True).reshape(NST, INNER)
-    start = jnp.where(live > 0, start, jnp.zeros_like(start))
-    start = start.reshape(NST, LANES, CHUNKS, CC).transpose(1, 2, 0, 3)
+
     tail = lax.dynamic_index_in_dim(every_tail, hit_owner[mine], 0, keepdims=False)
-    return start, jnp.where(live > 0, tail, jnp.zeros_like(tail))
-
-
-def local(
-    mesh, xbc, dt_raw, conv_weight, conv_bias, dt_bias, a_log, d_skip, cache_states, cache_tails,
-    hit_owner, hit_slot, hit_spans, request_of,
-):
-    rows = xbc.shape[0]
-    if mesh.shape["req"] == 16:
-        start, tail = fetch(mesh, cache_states, cache_tails, hit_owner, hit_slot, hit_spans, request_of)
-    else:
-        start, tail = fetch_any(cache_states, cache_tails, hit_owner, hit_slot, hit_spans, request_of)
-    tail = jnp.pad(tail.astype(jnp.float32), ((5, 0), (0, 0)))
+    tail = jnp.where(live > 0, tail, jnp.zeros_like(tail)).astype(jnp.float32)
+    tail = jnp.pad(tail, ((5, 0), (0, 0)))
     step = jax.nn.softplus(dt_raw + dt_bias[None, :])
     below = jnp.tril(jnp.ones((rows, rows), jnp.float32))
     cum = jnp.dot(below, step * (-jnp.exp(a_log))[None, :], precision=lax.Precision.HIGHEST)
@@ -657,14 +833,11 @@
             jax.ShapeDtypeStruct((rows, INNER), jnp.bfloat16),
             jax.ShapeDtypeStruct((1, NST, INNER), jnp.bfloat16),
         ),
-        in_specs=[
-            pl.BlockSpec((1, COLS // CC, NST, CC), lambda i: (i // 2, i % 2, 0, 0)),
-            wide(rows), wide(NST), group, tall, wide(1),
-        ],
+        in_specs=[pl.BlockSpec(memory_space=pltpu.SMEM), wide(NST), wide(rows), wide(NST), group, tall, wide(1)],
         out_specs=(wide(rows), pl.BlockSpec((1, NST, COLS), lambda i: (0, 0, i))),
         compiler_params=pltpu.CompilerParams(vmem_limit_bytes=58 * 2**20),
         name="state",
-    )(start, y_local, fresh, c_part, by_step(jnp.exp(cum)), elast)
+    )(live[None], start, y_local, fresh, c_part, by_step(jnp.exp(cum)), elast)
 
 
 def solution(mesh):
@@ -673,4 +846,5 @@
     in_specs = (
         rows, rows, P(), P(), P(), P(), P(), slots, slots, P("grp"), P("grp"), P("grp"), P(("grp", "req")),
     )
-    return jax.shard_map(functools.partial(local, mesh), mesh=mesh, in_specs=in_specs, out_specs=(rows, slots), check_vma=False)
+    body = functools.partial(local_routed, mesh) if mesh.shape["req"] == 16 else local
+    return jax.shard_map(body, mesh=mesh, in_specs=in_specs, out_specs=(rows, slots), check_vma=False)

time: 114 us -> 92 us (0.81)
  Pallas kernels: 98.6 us -> 82.3 us
  other arithmetic: 2.98 us -> 0 us
  local copies, waits for them, and re-layouts: 9.03 us -> 6.79 us
    pallas_call x2 -> x0, Pallas kernels: 21.8 us -> none  [the longest x1 13.3 us: local(): pl.pallas_call(local_kernel, grid=(STEPS,), out_shape=(jax.ShapeDtypeStru...]
    pallas_call x1, Pallas kernels: 66.7 us -> 72.2 us  [route(): pl.pallas_call(functools.partial(route_kernel, n, slots), out_shape=(jax....]
    reshape x4 -> x0, local copies, waits for them, and re-layouts: 3.09 us -> none  [the longest x3 3.04 us: by_step(): return a.reshape(a.shape[0], STEPS, PER_STEP).transpose(1, 0, 2)]
    unnamed x13 -> x10, local copies, waits for them, and re-layouts: 2.91 us -> 5.62 us
    another operation x2 -> x0, local copies, waits for them, and re-layouts: 1.46 us -> none  [the longest x1 0.74 us: local(): elast = jnp.repeat(jnp.exp(last), HEAD_DIM)[None, :]]
where the time goes in v2:
time: 92 us; the launch traced here: 91.7 us
  Pallas kernels  82.3 us (89%)
  local copies, waits for them, and re-layouts  6.79 us (7%)
  between operations  2.62 us (3%)
    pallas_call x1, Pallas kernels, route(): pl.pallas_call(functools.partial(route_kernel, n, slots), out_shape=(jax....  72.2 us
    pallas_call x1, Pallas kernels, info(): pl.pallas_call(functools.partial(info_kernel, groups, n), out_shape=jax.S...  10.1 us
    unnamed x10, local copies, waits for them, and re-layouts  5.62 us

profile of v2, /device:TPU:1, one launch (start us, length us, event | category | flops | bytes accessed | tf_op | source)
XLA Modules:
  0.0 91.7 jit_solution(8127865742702764161)
XLA Ops:
  1.3 0.0 copy-start
  1.3 0.6 copy-done
  1.9 0.0 copy-start.1
  1.9 0.7 copy-done.1
  2.6 0.0 copy-start.2
  2.6 0.7 copy-done.2
  3.2 10.1 %info.1 = s32[8,128]{1,0:T(8,128)S(1)} custom-call(s32[16]{0:T(128)S(1)} %copy-done, s32[16]{0:T(128)S(1)} %copy-done.1, s32[16]{0:T(128)S(1)} %copy-done.2, s32[1]{0:T(128)S(6)} %copy.29.request_ref), custom_call_target="tpu_custom_call" | custom-call | tf_op jit(solution)/shard_map/info/pallas_call | solution.py:222
  13.4 0.5 slice.3
  15.2 0.7 broadcast_in_dim.18
  15.8 72.2 %conditional.1 = ((bf16[128,8192]{1,0:T(8,128)(2,1)S(1)}, bf16[1,128,8192]{2,1,0:T(8,128)(2,1)})) conditional(s32[]{:T(128)} %bitcast, (s32[8,128]{1,0:T(8,128)S(1)}, bf16[3,128,8192]{2,1,0:T(8,128)(2,1)}, bf16[3,3,9216]{2,1,0:T(4,128)(2,1)}, bf16[128,9216]{1,0:T(8,128)(2,1)}, f32[128,128]{1,0:T(8,128)}, ...), branch_computations={%region_0.0_spmd, %region_1.0_spmd, %region_2.0_spmd} | conditional | bytes 8 | solution.py:754
  15.8 72.2 %route3.1 = (bf16[128,8192]{1,0:T(8,128)(2,1)S(1)}, bf16[1,128,8192]{2,1,0:T(8,128)(2,1)}) custom-call(s32[8,128]{1,0:T(8,128)S(1)} %get-tuple-element.60.tab, bf16[3,128,8192]{2,1,0:T(8,128)(2,1)} %get-tuple-element.61.states_ref, bf16[3,3,9216]{2,1,0:T(4,128)(2,1)} %get-tuple-element.62.tails_ref, bf16[128,9216]{1,0:T(8,128)(2,1)} %get-tuple-element.63.xbc_ref, ...), custom_call_target="tpu_custom_call" | custom-call | tf_op jit(solution)/shard_map/cond/branch_0_fun/route3/pallas_call | solution.py:713
  88.1 0.0 copy-start.3
  88.1 1.3 %copy.30 = bf16[128,8192]{1,0:T(8,128)(2,1)} copy(bf16[128,8192]{1,0:T(8,128)(2,1)S(1)} %get-tuple-element.108) | data formatting | bytes 4194304
  89.4 1.0 %copy-done.3 = bf16[1,128,8192]{2,1,0:T(8,128)(2,1)S(1)} copy-done((bf16[1,128,8192]{2,1,0:T(8,128)(2,1)S(1)}, bf16[1,128,8192]{2,1,0:T(8,128)(2,1)}, u32[]{:S(2)}) %copy-start.3) | copy-done | bytes 2097176
  90.4 1.3 %copy.31 = bf16[1,128,8192]{2,1,0:T(8,128)(2,1)} copy(bf16[1,128,8192]{2,1,0:T(8,128)(2,1)S(1)} %copy-done.3) | data formatting | bytes 4194304
Async XLA Ops:
  1.3 0.7 copy-start
  1.9 0.7 copy-start.1
  2.6 0.7 copy-start.2
  88.1 2.3 %copy-start.3 = (bf16[1,128,8192]{2,1,0:T(8,128)(2,1)S(1)}, bf16[1,128,8192]{2,1,0:T(8,128)(2,1)}, u32[]{:S(2)}) copy-start(bf16[1,128,8192]{2,1,0:T(8,128)(2,1)} %get-tuple-element.109) | copy-start | bytes 6291460
